TPU v7x, 32 devices: a whole 2x2x4 slice. The times are simulated.
32 devices in a mesh: blk: 16 (over z, y, x), rep: 2 (over core).
Axes of the slice: x: 2, y: 2, z: 4, core: 2. Of those that a mesh axis runs over, the one named last changes fastest.
Arguments:
- features: bfloat16 [4096, 256], P(('blk', 'rep')), may hold values from -6 to 6
- degrees: int32 [4096], P(('blk', 'rep')), may hold values from 4 to 64
- tile_values: bfloat16 [32, 4, 2, 128, 128], P(('blk', 'rep')), may hold values from 0 to 1
- tile_rows: int32 [32, 4, 2], P(('blk', 'rep')), may hold values from 0 to 1, as said below
- tile_counts: int32 [32, 4], P(('blk', 'rep')), may hold values from 1 to 2, as said below
- weight: bfloat16 [256, 256], replicated, may hold values from -0.375 to 0.375
- cotangent: bfloat16 [4096, 256], P(('blk', 'rep')), may hold values from -6 to 6
Outputs:
- activations: bfloat16 [4096, 256], P(('blk', 'rep'))
- grad_weight: float32 [256, 256], replicated
- grad_features: bfloat16 [4096, 256], P(('blk', 'rep'))
Inputs may be any that keep to these rules, and one draw needn't show every extreme that they name: `tile_rows`: the 2 slots of one owner and distance name the 2 row blocks of its slab, each once. Only the first tile_counts[o, s] slots of owner o and distance s are live. In every draw some slab has all 2 slots live at every distance for every owner in it.
All inputs are finite; a program needn't handle non-finite values.
Results may differ from a plain program's by a relative error of at most 0.0077.
Values may be sent and summed in bfloat16 or wider, within the bound.
A program may use at most 64 MiB of HBM per device.

v0:
```python
import math

import jax
import jax.numpy as jnp
from jax import lax
from jax.sharding import PartitionSpec as P


def passed_along(block, axis, distance):
    devices = range(lax.axis_size(axis))
    route = [((i - distance) % len(devices), i) for i in devices]
    return lax.ppermute(block, axis, route)


def per_device(features, degrees, tile_values, tile_rows, tile_counts, weight, cotangent):
    own_rows = features.shape[0]
    feature_width = features.shape[1]
    span_count = tile_values.shape[1]
    slot_count = tile_values.shape[2]
    block_size = tile_values.shape[3]
    inv_root = lax.rsqrt(degrees.astype(jnp.float32))[:, None]
    scaled = (features.astype(jnp.float32) * inv_root).astype(jnp.bfloat16)
    tile_stack = tile_values[0]
    row_stack = tile_rows[0]
    count_stack = tile_counts[0]
    slot_ids = jnp.arange(slot_count, dtype=jnp.int32)

    def load_distance(distance):
        tile_block = lax.dynamic_index_in_dim(tile_stack, distance, 0, keepdims=False)
        row_ids = lax.dynamic_index_in_dim(row_stack, distance, 0, keepdims=False)
        live_count = lax.dynamic_index_in_dim(count_stack, distance, 0, keepdims=False)
        return (tile_block, row_ids, live_count)

    def gather_rows(partial_sum, distance, source_rows):
        tile_block, row_ids, live_count = load_distance(distance)
        match_table = row_ids[None, :] == slot_ids[:, None]
        slot_of_row = jnp.sum(jnp.where(match_table, slot_ids[None, :], 0), axis=1)
        arranged = jnp.take(tile_block, slot_of_row, axis=0)
        row_live = slot_of_row < live_count
        product = jnp.einsum(
            "mij,jf->mif", arranged, source_rows, preferred_element_type=jnp.float32
        )
        return partial_sum + jnp.where(row_live[:, None, None], product, 0.0)

    def forward_turn(distance, carry):
        partial_sum, source_rows = carry
        partial_sum = gather_rows(partial_sum, distance, source_rows)
        source_rows = passed_along(source_rows, "blk", 1)
        return (partial_sum, source_rows)

    start_total = jnp.zeros((slot_count, block_size, feature_width), jnp.float32)
    partial_sum, source_rows = lax.fori_loop(0, span_count - 1, forward_turn, (start_total, scaled))
    partial_sum = gather_rows(partial_sum, span_count - 1, source_rows)
    slab_partial = partial_sum.reshape(slot_count * block_size, feature_width)
    own_sum = lax.psum_scatter(slab_partial, "rep", scatter_dimension=0, tiled=True)
    aggregated = (own_sum * inv_root).astype(jnp.bfloat16)
    pre_act = jnp.dot(aggregated, weight, preferred_element_type=jnp.float32)
    sigma = jax.nn.sigmoid(pre_act)
    activations = (pre_act * sigma).astype(jnp.bfloat16)
    act_grad = (cotangent.astype(jnp.float32) * sigma * (1.0 + pre_act * (1.0 - sigma))).astype(
        jnp.bfloat16
    )
    local_weight = lax.dot_general(
        aggregated, act_grad, (((0,), (0,)), ((), ())), preferred_element_type=jnp.float32
    )
    node_total = own_rows * lax.axis_size("blk") * lax.axis_size("rep")
    grad_weight = lax.psum(local_weight, ("blk", "rep")) / math.sqrt(node_total)
    back_grad = lax.dot_general(
        act_grad, weight, (((1,), (1,)), ((), ())), preferred_element_type=jnp.float32
    )
    back_scaled = (back_grad * inv_root).astype(jnp.bfloat16)
    slab_grads = lax.all_gather(back_scaled, "rep", axis=0, tiled=True).reshape(
        slot_count, block_size, feature_width
    )

    def scatter_rows(back_sum, distance):
        tile_block, row_ids, live_count = load_distance(distance)
        picked = jnp.take(slab_grads, row_ids, axis=0)
        picked = jnp.where((slot_ids < live_count)[:, None, None], picked, jnp.zeros_like(picked))
        return back_sum + jnp.einsum(
            "kij,kif->jf", tile_block, picked, preferred_element_type=jnp.float32
        )

    def backward_turn(turn_index, back_sum):
        back_sum = scatter_rows(back_sum, span_count - 1 - turn_index)
        return passed_along(back_sum, "blk", -1)

    zero_back = jnp.zeros((own_rows, feature_width), jnp.float32)
    back_total = lax.fori_loop(0, span_count - 1, backward_turn, zero_back)
    back_total = scatter_rows(back_total, 0)
    grad_features = (back_total * inv_root).astype(jnp.bfloat16)
    return (activations, grad_weight, grad_features)


def solution(mesh):
    placed = (
        P(("blk", "rep"), None),
        P(("blk", "rep")),
        P(("blk", "rep"), None, None, None, None),
        P(("blk", "rep"), None, None),
        P(("blk", "rep"), None),
        P(),
        P(("blk", "rep"), None),
    )
    return jax.shard_map(
        per_device,
        mesh=mesh,
        in_specs=placed,
        out_specs=(P(("blk", "rep"), None), P(), P(("blk", "rep"), None)),
        check_vma=False,
    )
```

profile of v0, /device:TPU:0, one launch (start us, length us, event | category | flops | bytes accessed | tf_op | source)
XLA Modules:
  0.0 186.1 jit_solution(1245400921345382711)
XLA Ops:
  7.9 1.0 slice_reduce_fusion
  8.8 0.8 copy.15
  9.7 1.3 fusion.42
  11.1 0.7 compare_and_fusion.3
  11.7 0.8 slice_bitcast_fusion
  12.6 0.9 multiply_convert_fusion.3
  14.1 0.6 copy-done.3
  14.7 24.9 %while.34 = (s32[]{:T(128)}, f32[2,128,256]{2,1,0:T(8,128)S(1)}, bf16[128,256]{1,0:T(8,128)(2,1)S(1)}, s32[4,2]{1,0:T(4,128)S(1)}, s32[4]{0:T(128)S(1)}, /*index...) while((s32[]{:T(128)}, f32[2,128,256]{2,1,0:T(8,128)S(1)}, ...), condition=%wide.region_2.4_spmd.clone.clone, body=%wide.region_0.3_spmd.clone.clone.sunk | while | flops 17007648 | bytes 1315055 | solution.py:52
  14.7 2.9 %collective-permute-start.1 = (bf16[128,256]{1,0:T(8,128)(2,1)S(1)}, bf16[128,256]{1,0:T(8,128)(2,1)S(1)}, u32[]{:S(2)}, u32[]{:S(2)}) collective-permute-start(bf16[128,256]{1,0:T(8,128)(2,1)S(1)} %copy.29), channel_id=1, source_target_pairs={{30,0},{0,2},{2,4},{4,6},{6,8},{8,10},{10,12},{12,14},{14,16},{16,... | collective-permute-start | bytes 196616 | tf_op jit(solution)/shard_map/while/body/eval_jaxpr/ppermute | solution.py:12
  18.4 0.7 compare_and_fusion.7
  19.9 4.0 %collective-permute-done.1 = bf16[128,256]{1,0:T(8,128)(2,1)S(1)} collective-permute-done((bf16[128,256]{1,0:T(8,128)(2,1)S(1)}, bf16[128,256]{1,0:T(8,128)(2,1)S(1)}, u32[]{:S(2)}, u32[]{:S(2)}) %collective-permute-start.1) | collective-permute-done | bytes 65568 | tf_op jit(solution)/shard_map/while/body/eval_jaxpr/ppermute | solution.py:12
  24.6 0.7 compare_and_fusion.7
  26.2 5.6 %collective-permute-done.1 = bf16[128,256]{1,0:T(8,128)(2,1)S(1)} collective-permute-done((bf16[128,256]{1,0:T(8,128)(2,1)S(1)}, bf16[128,256]{1,0:T(8,128)(2,1)S(1)}, u32[]{:S(2)}, u32[]{:S(2)}) %collective-permute-start.1) | collective-permute-done | bytes 65568 | tf_op jit(solution)/shard_map/while/body/eval_jaxpr/ppermute | solution.py:12
  32.5 0.7 compare_and_fusion.7
  34.1 5.6 %collective-permute-done.1 = bf16[128,256]{1,0:T(8,128)(2,1)S(1)} collective-permute-done((bf16[128,256]{1,0:T(8,128)(2,1)S(1)}, bf16[128,256]{1,0:T(8,128)(2,1)S(1)}, u32[]{:S(2)}, u32[]{:S(2)}) %collective-permute-start.1) | collective-permute-done | bytes 65568 | tf_op jit(solution)/shard_map/while/body/eval_jaxpr/ppermute | solution.py:12
  39.6 0.9 fusion.21
  40.7 0.7 compare_and_fusion.2
  41.3 3.0 %reduce-scatter.2.cloned.1.call-done = f32[128,256]{1,0:T(8,128)} async-done(((f32[256,256]{1,0:T(8,128)}), f32[128,256]{1,0:T(8,128)}) %reduce-scatter.2.cloned.1.call-update) | async-done | bytes 131088 | tf_op jit(solution)/shard_map/reduce_scatter | solution.py:55
  44.3 1.8 multiply_convert_fusion
  46.3 2.0 %all_gather.3 = bf16[256,256]{1,0:T(8,128)(2,1)S(1)} all-gather(bf16[128,256]{1,0:T(8,128)(2,1)S(1)} %fusion.25), channel_id=1, replica_groups=mesh['blk'=16,'rep'=2] {'rep'}, dimensions={0}, use_global_device_ids=true | all-gather | bytes 196608 | tf_op jit(solution)/shard_map/all_gather | solution.py:72
  48.3 1.0 fusion.40
  49.9 32.6 %while.33 = (s32[]{:T(128)}, f32[128,256]{1,0:T(8,128)S(1)}, bf16[4,2,128,128]{3,2,1,0:T(8,128)(2,1)S(1)}, s32[4]{0:T(128)S(1)}, s32[4,2]{1,0:T(4,128)S(1)}, /*i...) while((s32[]{:T(128)}, f32[128,256]{1,0:T(8,128)S(1)}, ...), condition=%wide.region_7.10_spmd.clone, body=%wide.region_6.9_spmd.clone.sunk | while | flops 16942100 | bytes 1250551 | solution.py:89
  50.6 0.6 compare_and_fusion.6
  52.0 5.4 %collective-permute-start = (f32[128,256]{1,0:T(8,128)S(1)}, f32[128,256]{1,0:T(8,128)S(1)}, u32[]{:S(2)}, u32[]{:S(2)}) collective-permute-start(f32[128,256]{1,0:T(8,128)S(1)} %fusion.54), channel_id=1, source_target_pairs={{2,0},{4,2},{6,4},{8,6},{10,8},{12,10},{14,12},{16,14},{18,16},{20... | collective-permute-start | bytes 393224 | tf_op jit(solution)/shard_map/while/body/eval_jaxpr/ppermute | solution.py:12
  57.4 3.4 %collective-permute-done = f32[128,256]{1,0:T(8,128)S(1)} collective-permute-done((f32[128,256]{1,0:T(8,128)S(1)}, f32[128,256]{1,0:T(8,128)S(1)}, u32[]{:S(2)}, u32[]{:S(2)}) %collective-permute-start) | collective-permute-done | bytes 131104 | tf_op jit(solution)/shard_map/while/body/eval_jaxpr/ppermute | solution.py:12
  62.9 6.3 %collective-permute-start = (f32[128,256]{1,0:T(8,128)S(1)}, f32[128,256]{1,0:T(8,128)S(1)}, u32[]{:S(2)}, u32[]{:S(2)}) collective-permute-start(f32[128,256]{1,0:T(8,128)S(1)} %fusion.54), channel_id=1, source_target_pairs={{2,0},{4,2},{6,4},{8,6},{10,8},{12,10},{14,12},{16,14},{18,16},{20... | collective-permute-start | bytes 393224 | tf_op jit(solution)/shard_map/while/body/eval_jaxpr/ppermute | solution.py:12
  69.1 2.6 %collective-permute-done = f32[128,256]{1,0:T(8,128)S(1)} collective-permute-done((f32[128,256]{1,0:T(8,128)S(1)}, f32[128,256]{1,0:T(8,128)S(1)}, u32[]{:S(2)}, u32[]{:S(2)}) %collective-permute-start) | collective-permute-done | bytes 131104 | tf_op jit(solution)/shard_map/while/body/eval_jaxpr/ppermute | solution.py:12
  73.8 6.2 %collective-permute-start = (f32[128,256]{1,0:T(8,128)S(1)}, f32[128,256]{1,0:T(8,128)S(1)}, u32[]{:S(2)}, u32[]{:S(2)}) collective-permute-start(f32[128,256]{1,0:T(8,128)S(1)} %fusion.54), channel_id=1, source_target_pairs={{2,0},{4,2},{6,4},{8,6},{10,8},{12,10},{14,12},{16,14},{18,16},{20... | collective-permute-start | bytes 393224 | tf_op jit(solution)/shard_map/while/body/eval_jaxpr/ppermute | solution.py:12
  80.0 2.5 %collective-permute-done = f32[128,256]{1,0:T(8,128)S(1)} collective-permute-done((f32[128,256]{1,0:T(8,128)S(1)}, f32[128,256]{1,0:T(8,128)S(1)}, u32[]{:S(2)}, u32[]{:S(2)}) %collective-permute-start) | collective-permute-done | bytes 131104 | tf_op jit(solution)/shard_map/while/body/eval_jaxpr/ppermute | solution.py:12
  82.5 0.9 fusion.24
  83.4 94.2 %all-reduce.2.cloned.1.call-done = f32[256,256]{1,0:T(8,128)} async-done(((f32[256,256]{1,0:T(8,128)}), f32[256,256]{1,0:T(8,128)}) %all-reduce.2.cloned.1.call-update) | async-done | bytes 262160 | tf_op jit(solution)/shard_map/psum | solution.py:67
  177.6 1.7 broadcast_multiply_fusion
  (69 shorter events, 12.5 us)
Async XLA Ops:
  7.2 37.1 %copy-start = (bf16[256,256]{1,0:T(8,128)(2,1)S(1)}, bf16[256,256]{1,0:T(8,128)(2,1)}, u32[]{:S(2)}) copy-start(bf16[256,256]{1,0:T(8,128)(2,1)} %param.20) | copy-start | bytes 393220
  7.2 0.7 copy-start.5
  7.2 6.9 %copy-start.1 = (bf16[1,4,2,128,128]{4,3,2,1,0:T(8,128)(2,1)S(1)}, bf16[1,4,2,128,128]{4,3,2,1,0:T(8,128)(2,1)}, u32[]{:S(2)}) copy-start(bf16[1,4,2,128,128]{4,3,2,1,0:T(8,128)(2,1)} %param.17) | copy-start | bytes 786436
  7.2 37.1 %reduce-scatter.2.cloned.1.call-start = ((), (), s32[]{:S(2)}) async-start(), calls=%async_computation.1 | async-start | bytes 393216 | tf_op jit(solution)/shard_map/reduce_scatter | solution.py:55
  14.1 0.7 copy-start.3
  14.7 9.2 %collective-permute-start.1 = (bf16[128,256]{1,0:T(8,128)(2,1)S(1)}, bf16[128,256]{1,0:T(8,128)(2,1)S(1)}, u32[]{:S(2)}, u32[]{:S(2)}) collective-permute-start(bf16[128,256]{1,0:T(8,128)(2,1)S(1)} %copy.29), channel_id=1, source_target_pairs={{30,0},{0,2},{2,4},{4,6},{6,8},{8,10},{10,12},{12,14},{14,16},{16,... | collective-permute-start | bytes 196616 | tf_op jit(solution)/shard_map/while/body/eval_jaxpr/ppermute | solution.py:12
  23.9 7.9 %collective-permute-start.1 = (bf16[128,256]{1,0:T(8,128)(2,1)S(1)}, bf16[128,256]{1,0:T(8,128)(2,1)S(1)}, u32[]{:S(2)}, u32[]{:S(2)}) collective-permute-start(bf16[128,256]{1,0:T(8,128)(2,1)S(1)} %copy.29), channel_id=1, source_target_pairs={{30,0},{0,2},{2,4},{4,6},{6,8},{8,10},{10,12},{12,14},{14,16},{16,... | collective-permute-start | bytes 196616 | tf_op jit(solution)/shard_map/while/body/eval_jaxpr/ppermute | solution.py:12
  31.8 7.9 %collective-permute-start.1 = (bf16[128,256]{1,0:T(8,128)(2,1)S(1)}, bf16[128,256]{1,0:T(8,128)(2,1)S(1)}, u32[]{:S(2)}, u32[]{:S(2)}) collective-permute-start(bf16[128,256]{1,0:T(8,128)(2,1)S(1)} %copy.29), channel_id=1, source_target_pairs={{30,0},{0,2},{2,4},{4,6},{6,8},{8,10},{10,12},{12,14},{14,16},{16,... | collective-permute-start | bytes 196616 | tf_op jit(solution)/shard_map/while/body/eval_jaxpr/ppermute | solution.py:12
  40.6 3.7 %copy-start.4 = (bf16[128,256]{1,0:T(8,128)(2,1)S(1)}, bf16[128,256]{1,0:T(8,128)(2,1)}, u32[]{:S(2)}) copy-start(bf16[128,256]{1,0:T(8,128)(2,1)} %param.21) | copy-start | bytes 196612
  40.6 137.0 %all-reduce.2.cloned.1.call-start = ((), (), s32[]{:S(2)}) async-start(), calls=%async_computation.2 | async-start | bytes 524288 | tf_op jit(solution)/shard_map/psum | solution.py:67
  46.3 2.0 %copy-start.2 = (f32[128,256]{1,0:T(8,128)S(1)}, f32[128,256]{1,0:T(8,128)}, u32[]{:S(2)}) copy-start(f32[128,256]{1,0:T(8,128)} %reduce-scatter.2.cloned.1.call-done) | copy-start | bytes 393220
  52.0 8.8 %collective-permute-start = (f32[128,256]{1,0:T(8,128)S(1)}, f32[128,256]{1,0:T(8,128)S(1)}, u32[]{:S(2)}, u32[]{:S(2)}) collective-permute-start(f32[128,256]{1,0:T(8,128)S(1)} %fusion.54), channel_id=1, source_target_pairs={{2,0},{4,2},{6,4},{8,6},{10,8},{12,10},{14,12},{16,14},{18,16},{20... | collective-permute-start | bytes 393224 | tf_op jit(solution)/shard_map/while/body/eval_jaxpr/ppermute | solution.py:12
  62.9 8.9 %collective-permute-start = (f32[128,256]{1,0:T(8,128)S(1)}, f32[128,256]{1,0:T(8,128)S(1)}, u32[]{:S(2)}, u32[]{:S(2)}) collective-permute-start(f32[128,256]{1,0:T(8,128)S(1)} %fusion.54), channel_id=1, source_target_pairs={{2,0},{4,2},{6,4},{8,6},{10,8},{12,10},{14,12},{16,14},{18,16},{20... | collective-permute-start | bytes 393224 | tf_op jit(solution)/shard_map/while/body/eval_jaxpr/ppermute | solution.py:12
  73.8 8.7 %collective-permute-start = (f32[128,256]{1,0:T(8,128)S(1)}, f32[128,256]{1,0:T(8,128)S(1)}, u32[]{:S(2)}, u32[]{:S(2)}) collective-permute-start(f32[128,256]{1,0:T(8,128)S(1)} %fusion.54), channel_id=1, source_target_pairs={{2,0},{4,2},{6,4},{8,6},{10,8},{12,10},{14,12},{16,14},{18,16},{20... | collective-permute-start | bytes 393224 | tf_op jit(solution)/shard_map/while/body/eval_jaxpr/ppermute | solution.py:12
Sparse Core Ops, SparseCore 0:
  40.7 3.5 reduce-scatter.1
  51.3 126.2 all-reduce.1
where the time goes:
time: 187 us; the launch traced here: 186 us
  waiting for transfers between devices  121 us (65%)
  starting transfers between devices  20.9 us (11%)
  between operations  14.2 us (8%)
  local copies, waits for them, and re-layouts  13.3 us (7%)
  other arithmetic  8.29 us (4%)
  matrix products  6.37 us (3%)
  blocking collectives  2.03 us (1%)
    psum x1, waiting for transfers between devices, per_device(): grad_weight = lax.psum(local_weight, ('blk', 'rep')) / math.sqrt(node_total)  94.2 us
    ppermute x6, waiting for transfers between devices, passed_along(): return lax.ppermute(block, axis, route)  23.6 us
    ppermute x6, starting transfers between devices, passed_along(): return lax.ppermute(block, axis, route)  20.8 us
    dynamic_slice x7, local copies, waits for them, and re-layouts, load_distance(): lax.dynamic_index_in_dim(count_stack, distance, 0, keepdims=False)  4.86 us
  transfers between devices with their start and end apart: 8, of which 8 were waited for; matrix products, arithmetic and copies ran while one was open for 8% of the time, Pallas kernels for 0%

commit v1 on v0

v1 whole, which is shorter than its diff:
```python
import functools
import math

import jax
import jax.numpy as jnp
from jax import lax
from jax.experimental import pallas as pl
from jax.experimental.pallas import tpu as pltpu
from jax.sharding import PartitionSpec as P

F32 = jnp.float32
BF16 = jnp.bfloat16
MESH = pl.DeviceIdType.MESH
GROUP = 4


def dot(a, b, ca, cb):
    return lax.dot_general(a, b, (((ca,), (cb,)), ((), ())), preferred_element_type=F32)


def fused_kernel(dims, *refs):
    n_blk, n_rep, span, cap, bs, own, width, nodes, reduce_here = dims
    (feat_hbm, deg_hbm, tile_hbm, rows_hbm, counts_hbm, w_hbm, cot_hbm,
     act_hbm, gw_hbm, gf_hbm,
     feat, deg, tiles, rows_s, counts_s, weight, cot, scaled, source, adj, part,
     agg, act_all, gact, back, inv, bpart, bpart_in, gf, gwf, gwb, ring1, ring2, gw_all,
     load_sem, fwd_send, fwd_recv, rep_send, rep_recv, bwd_send, bwd_recv,
     r1_send, r1_recv, r2_send, r2_recv, r3_send, r3_recv, out_sem) = refs
    slab = cap * bs
    depth = n_blk // GROUP
    me = lax.axis_index("blk")
    core = lax.axis_index("rep")

    def at_distance(s):
        return lax.rem(me + s + n_blk, n_blk)

    def at_core(u):
        return lax.rem(core + u, n_rep)

    plane = (me // GROUP) * GROUP
    spot = lax.rem(me, GROUP)

    def in_plane(t):
        return plane + lax.rem(spot + t, GROUP)

    barrier = pltpu.get_barrier_semaphore()
    peers = [(at_distance(s), core) for d in range(1, span) for s in (d, -d)]
    peers += [(me, at_core(u)) for u in range(1, n_rep)]
    if reduce_here:
        peers += [(in_plane(t), at_core(u)) for t in range(1, GROUP) for u in range(n_rep)]
        peers += [(at_distance(GROUP * t), core) for t in range(1, depth)]
    for peer in peers:
        pl.semaphore_signal(barrier, inc=1, device_id=peer, device_id_type=MESH)

    def load(src, dst, i):
        copy = pltpu.make_async_copy(src, dst, load_sem.at[i])
        copy.start()
        return copy

    mine = pl.ds(pl.multiple_of(core * own, own), own)
    loads = [
        load(deg_hbm, deg.at[core], 0),
        load(feat_hbm, feat, 1),
        load(rows_hbm, rows_s, 2),
        load(counts_hbm, counts_s, 3),
        load(tile_hbm, tiles, 4),
        load(cot_hbm, cot.at[core], 5),
        load(w_hbm, weight, 6),
    ]
    loads[0].wait()
    loads[1].wait()

    def column(row):
        block = jnp.broadcast_to(lax.rsqrt(row.astype(F32)), (own, own)).T
        return jnp.concatenate([block] * (width // own), axis=1)

    scaled[...] = (feat[...].astype(F32) * column(deg[core])).astype(BF16)
    pl.semaphore_wait(barrier, len(peers))

    def remote(src, dst, send, recv, peer):
        copy = pltpu.make_async_remote_copy(
            src_ref=src, dst_ref=dst, send_sem=send, recv_sem=recv,
            device_id=peer, device_id_type=MESH)
        copy.start()
        return copy

    forward = [
        remote(scaled, source.at[s - 1], fwd_send.at[s - 1], fwd_recv.at[s - 1], (at_distance(s), core))
        for s in range(span - 1, 0, -1)
    ][::-1]
    loads[5].wait()
    early = []
    for u in range(1, n_rep):
        peer = (me, at_core(u))
        early.append(remote(deg.at[core], deg.at[core], rep_send.at[0, u - 1], rep_recv.at[0, u - 1], peer))
        early.append(remote(cot.at[core], cot.at[core], rep_send.at[1, u - 1], rep_recv.at[1, u - 1], peer))
    loads[2].wait()
    loads[3].wait()
    loads[4].wait()

    def arrange(s, m):
        slot = jnp.int32(0)
        for k in range(cap):
            slot = jnp.where(rows_s[0, s, k] == m, k, slot)
        tile = tiles[0, s, slot]
        live = jnp.broadcast_to(slot < counts_s[0, s], tile.shape)
        return jnp.where(live, tile, jnp.zeros_like(tile))

    if span * cap <= 16:
        for s in range(span):
            for m in range(cap):
                adj[s, m * bs:(m + 1) * bs, :] = arrange(s, m)
    else:
        def arrange_one(i, carry):
            s = i // cap
            m = lax.rem(i, cap)
            adj[s, pl.ds(pl.multiple_of(m * bs, bs), bs), :] = arrange(s, m)
            return carry
        lax.fori_loop(0, span * cap, arrange_one, 0)

    part[core] = dot(adj[0], scaled[...], 1, 0)
    for s in range(1, span):
        forward[s - 1].wait_recv()
        part[core] += dot(adj[s], source[s - 1], 1, 0)
    exchange = [
        remote(part.at[core], part.at[core], rep_send.at[2, u - 1], rep_recv.at[2, u - 1], (me, at_core(u)))
        for u in range(1, n_rep)
    ]
    loads[6].wait()
    for copy in early:
        copy.wait_recv()
    for r in range(n_rep):
        inv[r * own:(r + 1) * own, :] = column(deg[r])
    for copy in exchange:
        copy.wait_recv()
    total = part[0]
    for r in range(1, n_rep):
        total = total + part[r]
    inv_root = inv[...]
    aggregated = (total * inv_root).astype(BF16)
    agg[...] = aggregated
    pre_act = jnp.dot(aggregated, weight[...], preferred_element_type=F32)
    sigma = jax.nn.sigmoid(pre_act)
    act_all[...] = (pre_act * sigma).astype(BF16)
    seed = cot[...].reshape(slab, width).astype(F32)
    act_grad = (seed * sigma * (1.0 + pre_act * (1.0 - sigma))).astype(BF16)
    gact[...] = act_grad
    scale = 1.0 / math.sqrt(nodes)
    if reduce_here:
        cols = width // n_rep
        piece = cols // GROUP
        half = agg[:, pl.ds(pl.multiple_of(core * cols, cols), cols)]
        local_weight = dot(half, act_grad, 0, 0) * scale
        gwf[...] = local_weight
        gwb[...] = local_weight.astype(BF16)
        first = []
        for t in range(1, GROUP):
            rows = pl.ds(pl.multiple_of(lax.rem(spot + t, GROUP) * piece, piece), piece)
            first.append(remote(gwb.at[rows], ring1.at[t - 1], r1_send.at[t - 1], r1_recv.at[t - 1],
                                (in_plane(t), core)))
    else:
        gwf[...] = dot(agg[mine, :], gact[mine, :], 0, 0) * scale
    back[...] = (dot(gact[...], weight[...], 1, 1) * inv_root).astype(BF16)
    backward = []
    for s in range(1, span):
        bpart[s - 1] = dot(adj[s], back[...], 0, 0).astype(BF16)
        backward.append(remote(bpart.at[s - 1], bpart_in.at[s - 1], bwd_send.at[s - 1], bwd_recv.at[s - 1],
                               (at_distance(-s), core)))
    outs = [pltpu.make_async_copy(act_all.at[mine], act_hbm, out_sem.at[0])]
    outs[0].start()
    own_back = dot(adj[0], back[...], 0, 0)
    if reduce_here:
        own_rows = pl.ds(pl.multiple_of(spot * piece, piece), piece)
        reduced = gwf[own_rows, :]
        for t in range(1, GROUP):
            first[t - 1].wait_recv()
            reduced = reduced + ring1[t - 1].astype(F32)
        level = me // GROUP
        ring2[level] = reduced.astype(BF16)
        second = [
            remote(ring2.at[level], ring2.at[level], r2_send.at[t - 1], r2_recv.at[t - 1],
                   (at_distance(GROUP * t), core))
            for t in range(1, depth)
        ]
        for copy in second:
            copy.wait_recv()
        whole = ring2[0].astype(F32)
        for t in range(1, depth):
            whole = whole + ring2[t].astype(F32)
        final_rows = pl.ds(pl.multiple_of(core * cols + spot * piece, piece), piece)
        gw_all[final_rows, :] = whole.astype(BF16)
        third = []
        for t in range(GROUP):
            for u in range(n_rep):
                if t or u:
                    i = t * n_rep + u - 1
                    third.append(remote(gw_all.at[final_rows], gw_all.at[final_rows], r3_send.at[i],
                                        r3_recv.at[i], (in_plane(t), at_core(u))))
    for s in range(1, span):
        backward[s - 1].wait_recv()
        own_back = own_back + bpart_in[s - 1].astype(F32)
    gf[...] = (own_back * inv[mine, :]).astype(BF16)
    outs.append(pltpu.make_async_copy(gf, gf_hbm, out_sem.at[1]))
    outs[1].start()
    if reduce_here:
        for copy in third:
            copy.wait_recv()
        outs.append(pltpu.make_async_copy(gw_all, gw_hbm, out_sem.at[2]))
    else:
        outs.append(pltpu.make_async_copy(gwf, gw_hbm, out_sem.at[2]))
    outs[2].start()
    sent = forward + early + exchange + backward
    if reduce_here:
        sent += first + second + third
    for copy in sent:
        copy.wait_send()
    for copy in outs:
        copy.wait()


def per_device(n_blk, n_rep, features, degrees, tile_values, tile_rows, tile_counts, weight, cotangent):
    own, width = features.shape
    _, span, cap, bs, _ = tile_values.shape
    nodes = own * n_blk * n_rep
    slab = cap * bs
    cols = width // n_rep
    reduce_here = n_blk % GROUP == 0 and n_blk // GROUP <= 4 and cols % 128 == 0
    piece = cols // GROUP
    depth = n_blk // GROUP
    dims = (n_blk, n_rep, span, cap, bs, own, width, nodes, reduce_here)
    gw_rows = cols if reduce_here else width
    dma = pltpu.SemaphoreType.DMA
    scratch = [
        pltpu.VMEM((own, width), BF16),
        pltpu.VMEM((n_rep, 1, own), jnp.int32),
        pltpu.VMEM(tile_values.shape, BF16),
        pltpu.SMEM(tile_rows.shape, jnp.int32),
        pltpu.SMEM(tile_counts.shape, jnp.int32),
        pltpu.VMEM((width, width), BF16),
        pltpu.VMEM((n_rep, own, width), BF16),
        pltpu.VMEM((own, width), BF16),
        pltpu.VMEM((span - 1, own, width), BF16),
        pltpu.VMEM((span, slab, bs), BF16),
        pltpu.VMEM((n_rep, slab, width), F32),
        pltpu.VMEM((slab, width), BF16),
        pltpu.VMEM((slab, width), BF16),
        pltpu.VMEM((slab, width), BF16),
        pltpu.VMEM((slab, width), BF16),
        pltpu.VMEM((slab, width), F32),
        pltpu.VMEM((span - 1, own, width), BF16),
        pltpu.VMEM((span - 1, own, width), BF16),
        pltpu.VMEM((own, width), BF16),
        pltpu.VMEM((gw_rows, width), F32),
        pltpu.VMEM((gw_rows, width), BF16),
        pltpu.VMEM((GROUP - 1, max(piece, 16), width), BF16),
        pltpu.VMEM((max(depth, 1), max(piece, 16), width), BF16),
        pltpu.VMEM((width, width), BF16),
        dma((7,)),
        dma((span - 1,)), dma((span - 1,)),
        dma((3, n_rep - 1)), dma((3, n_rep - 1)),
        dma((span - 1,)), dma((span - 1,)),
        dma((GROUP - 1,)), dma((GROUP - 1,)),
        dma((max(depth - 1, 1),)), dma((max(depth - 1, 1),)),
        dma((GROUP * n_rep - 1,)), dma((GROUP * n_rep - 1,)),
        dma((3,)),
    ]
    anywhere = pl.BlockSpec(memory_space=pl.ANY)
    activations, grad_weight, grad_features = pl.pallas_call(
        functools.partial(fused_kernel, dims),
        out_shape=(
            jax.ShapeDtypeStruct((own, width), BF16),
            jax.ShapeDtypeStruct((width, width), BF16 if reduce_here else F32),
            jax.ShapeDtypeStruct((own, width), BF16),
        ),
        in_specs=[anywhere] * 7,
        out_specs=(anywhere,) * 3,
        scratch_shapes=scratch,
        compiler_params=pltpu.CompilerParams(
            collective_id=0, has_side_effects=True, vmem_limit_bytes=48 * 1024 * 1024),
    )(features, degrees.reshape(1, own), tile_values, tile_rows, tile_counts, weight, cotangent)
    if reduce_here:
        grad_weight = grad_weight.astype(F32)
    else:
        grad_weight = lax.psum(grad_weight, ("blk", "rep"))
    return (activations, grad_weight, grad_features)


def solution(mesh):
    placed = (
        P(("blk", "rep"), None),
        P(("blk", "rep")),
        P(("blk", "rep"), None, None, None, None),
        P(("blk", "rep"), None, None),
        P(("blk", "rep"), None),
        P(),
        P(("blk", "rep"), None),
    )
    return jax.shard_map(
        functools.partial(per_device, mesh.shape["blk"], mesh.shape["rep"]),
        mesh=mesh,
        in_specs=placed,
        out_specs=(P(("blk", "rep"), None), P(), P(("blk", "rep"), None)),
        check_vma=False,
    )
```

time: 187 us -> 32.1 us (0.17)
  waiting for transfers between devices: 121 us -> 0 us
  Pallas kernels: 0 us -> 24.3 us
  starting transfers between devices: 20.9 us -> 0 us
  between operations: 14.2 us -> 0.66 us
  other arithmetic: 8.29 us -> 0.72 us
  local copies, waits for them, and re-layouts: 13.3 us -> 6.13 us
  matrix products: 6.37 us -> 0 us
  blocking collectives: 2.03 us -> 0 us
    psum x1 -> x0, waiting for transfers between devices: 94.2 us -> none  [per_device(): grad_weight = lax.psum(local_weight, ('blk', 'rep')) / math.sqrt(node_total)]
    pallas_call x0 -> x1, Pallas kernels: none -> 24.3 us  [per_device(): pl.pallas_call(functools.partial(fused_kernel, dims), out_shape=(jax.Shap...]
    ppermute x6 -> x0, waiting for transfers between devices: 23.6 us -> none  [passed_along(): return lax.ppermute(block, axis, route)]
    ppermute x6 -> x0, starting transfers between devices: 20.8 us -> none  [passed_along(): return lax.ppermute(block, axis, route)]
    dot_general x11 -> x0, matrix products: 6.37 us -> none  [the longest x1 1.8 us: per_device(): pre_act = jnp.dot(aggregated, weight, preferred_element_type=jnp.float32)]
    dynamic_slice x8 -> x0, local copies, waits for them, and re-layouts: 5.83 us -> none  [the longest x7 4.86 us: load_distance(): lax.dynamic_index_in_dim(count_stack, distance, 0, keepdims=False)]
    and x8 -> x0, other arithmetic: 5.16 us -> none  [the longest x4 2.6 us: gather_rows(): arranged = jnp.take(tile_block, slot_of_row, axis=0)]
    gather x8 -> x0, local copies, waits for them, and re-layouts: 4.48 us -> none  [the longest x4 2.25 us: gather_rows(): arranged = jnp.take(tile_block, slot_of_row, axis=0)]
  transfers between devices with their start and end apart: 8 -> 0, of which waited for: 8 -> 0; matrix products, arithmetic and copies ran while one was open for 8% -> 0% of each run, Pallas kernels for 0% -> 0%
where the time goes in v1:
time: 32.1 us; the launch traced here: 31.8 us
  Pallas kernels  24.3 us (76%)
  local copies, waits for them, and re-layouts  6.13 us (19%)
  other arithmetic  0.72 us (2%)
  between operations  0.66 us (2%)
    pallas_call x1, Pallas kernels, per_device(): pl.pallas_call(functools.partial(fused_kernel, dims), out_shape=(jax.Shap...  24.3 us
    unnamed x17, local copies, waits for them, and re-layouts  6.13 us
    convert_element_type x1, other arithmetic, per_device(): grad_weight = grad_weight.astype(F32)  0.72 us

profile of v1, /device:TPU:0, one launch (start us, length us, event | category | flops | bytes accessed | tf_op | source)
XLA Modules:
  0.0 31.8 jit_solution(2050354940754892363)
XLA Ops:
  0.6 0.0 copy-start.6
  0.6 0.7 %copy-done.6 = s32[1,4,2]{1,2,0:T(2,128)S(1)} copy-done((s32[1,4,2]{1,2,0:T(2,128)S(1)}, s32[1,4,2]{1,2,0:T(2,128)}, u32[]{:S(2)}) %copy-start.6) | copy-done | bytes 56
  1.3 0.0 copy-start.4
  1.3 0.0 copy-start.5
  1.3 0.1 copy.10.refs_3_
  1.4 0.6 %copy-done.4 = s32[128]{0:T(128)S(1)} copy-done((s32[128]{0:T(128)S(1)}, s32[128]{0:T(128)}, u32[]{:S(2)}) %copy-start.4) | copy-done | bytes 536
  2.0 0.0 copy-done.5
  2.0 0.0 copy-start
  2.0 0.9 %copy-done = bf16[1,4,2,128,128]{4,3,2,1,0:T(8,128)(2,1)S(1)} copy-done((bf16[1,4,2,128,128]{4,3,2,1,0:T(8,128)(2,1)S(1)}, bf16[1,4,2,128,128]{4,3,2,1,0:T(8,128)(2,1)}, u32[]{:S(2)}) %copy-start) | copy-done | bytes 262168
  2.9 0.0 copy-start.1
  2.9 0.9 %copy-done.1 = bf16[256,256]{1,0:T(8,128)(2,1)S(1)} copy-done((bf16[256,256]{1,0:T(8,128)(2,1)S(1)}, bf16[256,256]{1,0:T(8,128)(2,1)}, u32[]{:S(2)}) %copy-start.1) | copy-done | bytes 131096
  3.8 0.0 copy-start.2
  3.8 0.8 %copy-done.2 = bf16[128,256]{1,0:T(8,128)(2,1)S(1)} copy-done((bf16[128,256]{1,0:T(8,128)(2,1)S(1)}, bf16[128,256]{1,0:T(8,128)(2,1)}, u32[]{:S(2)}) %copy-start.2) | copy-done | bytes 65560
  4.7 0.0 copy-start.3
  4.7 0.8 %copy-done.3 = bf16[128,256]{1,0:T(8,128)(2,1)S(1)} copy-done((bf16[128,256]{1,0:T(8,128)(2,1)S(1)}, bf16[128,256]{1,0:T(8,128)(2,1)}, u32[]{:S(2)}) %copy-start.3) | copy-done | bytes 65560
  5.5 24.3 %shard_map.94 = (bf16[128,256]{1,0:T(8,128)(2,1)S(1)}, bf16[256,256]{1,0:T(8,128)(2,1)S(1)}, bf16[128,256]{1,0:T(8,128)(2,1)S(1)}) custom-call(bf16[128,256]{1,0:T(8,128)(2,1)S(1)} %copy-done.2, s32[1,128]{1,0:T(1,128)S(1)} %bitcast.1, bf16[1,4,2,128,128]{4,3,2,1,0:T(8,128)(2,1)S(1)} %copy-done, s32[1,4,2]{2,1,0:T(4,128)S(1)} %copy.10.refs_3_, ...), custom_call_target="tpu_custom_call" | custom-call | tf_op jit(solution)/shard_map/pallas_call | solution.py:268
  29.8 0.7 %convert_element_type.3 = f32[256,256]{1,0:T(8,128)} convert(bf16[256,256]{1,0:T(8,128)(2,1)S(1)} %get-tuple-element.7) | non-fusion elementwise | flops 65536 | bytes 393216 | tf_op jit(solution)/shard_map/convert_element_type | solution.py:282
  30.5 0.6 %copy.13 = bf16[128,256]{1,0:T(8,128)(2,1)} copy(bf16[128,256]{1,0:T(8,128)(2,1)S(1)} %get-tuple-element.12) | data formatting | bytes 131072
  31.2 0.6 %copy.14 = bf16[128,256]{1,0:T(8,128)(2,1)} copy(bf16[128,256]{1,0:T(8,128)(2,1)S(1)} %get-tuple-element.14) | data formatting | bytes 131072
Async XLA Ops:
  0.6 0.7 %copy-start.6 = (s32[1,4,2]{1,2,0:T(2,128)S(1)}, s32[1,4,2]{1,2,0:T(2,128)}, u32[]{:S(2)}) copy-start(s32[1,4,2]{1,2,0:T(2,128)} %param.10) | copy-start | bytes 100
  1.3 0.7 %copy-start.4 = (s32[128]{0:T(128)S(1)}, s32[128]{0:T(128)}, u32[]{:S(2)}) copy-start(s32[128]{0:T(128)} %param.8) | copy-start | bytes 1540
  1.3 0.7 %copy-start.5 = (s32[1,4]{1,0:T(1,128)S(1)}, s32[1,4]{1,0:T(1,128)}, u32[]{:S(2)}) copy-start(s32[1,4]{1,0:T(1,128)} %refs_4_.1) | copy-start | bytes 52
  2.0 0.9 %copy-start = (bf16[1,4,2,128,128]{4,3,2,1,0:T(8,128)(2,1)S(1)}, bf16[1,4,2,128,128]{4,3,2,1,0:T(8,128)(2,1)}, u32[]{:S(2)}) copy-start(bf16[1,4,2,128,128]{4,3,2,1,0:T(8,128)(2,1)} %refs_2_.1) | copy-start | bytes 786436
  2.9 0.9 %copy-start.1 = (bf16[256,256]{1,0:T(8,128)(2,1)S(1)}, bf16[256,256]{1,0:T(8,128)(2,1)}, u32[]{:S(2)}) copy-start(bf16[256,256]{1,0:T(8,128)(2,1)} %refs_5_.1) | copy-start | bytes 393220
  3.8 0.8 %copy-start.2 = (bf16[128,256]{1,0:T(8,128)(2,1)S(1)}, bf16[128,256]{1,0:T(8,128)(2,1)}, u32[]{:S(2)}) copy-start(bf16[128,256]{1,0:T(8,128)(2,1)} %refs_0_.1) | copy-start | bytes 196612
  4.7 0.8 %copy-start.3 = (bf16[128,256]{1,0:T(8,128)(2,1)S(1)}, bf16[128,256]{1,0:T(8,128)(2,1)}, u32[]{:S(2)}) copy-start(bf16[128,256]{1,0:T(8,128)(2,1)} %refs_6_.1) | copy-start | bytes 196612

commit v2 on v1

--- a/solution.py
+++ b/solution.py
@@ -21,11 +21,11 @@
 def fused_kernel(dims, *refs):
     n_blk, n_rep, span, cap, bs, own, width, nodes, reduce_here = dims
     (feat_hbm, deg_hbm, tile_hbm, rows_hbm, counts_hbm, w_hbm, cot_hbm,
-     act_hbm, gw_hbm, gf_hbm,
+     act_out, gw_out, gf_out,
      feat, deg, tiles, rows_s, counts_s, weight, cot, scaled, source, adj, part,
-     agg, act_all, gact, back, inv, bpart, bpart_in, gf, gwf, gwb, ring1, ring2, gw_all,
+     agg, act_all, gact, back, inv, bpart, bpart_in, gwf, gwb, ring1, ring2, gw_all,
      load_sem, fwd_send, fwd_recv, rep_send, rep_recv, bwd_send, bwd_recv,
-     r1_send, r1_recv, r2_send, r2_recv, r3_send, r3_recv, out_sem) = refs
+     r1_send, r1_recv, r2_send, r2_recv, r3_send, r3_recv) = refs
     slab = cap * bs
     depth = n_blk // GROUP
     me = lax.axis_index("blk")
@@ -101,7 +101,7 @@
     def arrange(s, m):
         slot = jnp.int32(0)
         for k in range(cap):
-            slot = jnp.where(rows_s[0, s, k] == m, k, slot)
+            slot = jnp.where(rows_s[0, k, s] == m, k, slot)
         tile = tiles[0, s, slot]
         live = jnp.broadcast_to(slot < counts_s[0, s], tile.shape)
         return jnp.where(live, tile, jnp.zeros_like(tile))
@@ -166,8 +166,7 @@
         bpart[s - 1] = dot(adj[s], back[...], 0, 0).astype(BF16)
         backward.append(remote(bpart.at[s - 1], bpart_in.at[s - 1], bwd_send.at[s - 1], bwd_recv.at[s - 1],
                                (at_distance(-s), core)))
-    outs = [pltpu.make_async_copy(act_all.at[mine], act_hbm, out_sem.at[0])]
-    outs[0].start()
+    act_out[...] = act_all[mine, :]
     own_back = dot(adj[0], back[...], 0, 0)
     if reduce_here:
         own_rows = pl.ds(pl.multiple_of(spot * piece, piece), piece)
@@ -199,22 +198,26 @@
     for s in range(1, span):
         backward[s - 1].wait_recv()
         own_back = own_back + bpart_in[s - 1].astype(F32)
-    gf[...] = (own_back * inv[mine, :]).astype(BF16)
-    outs.append(pltpu.make_async_copy(gf, gf_hbm, out_sem.at[1]))
-    outs[1].start()
+    gf_out[...] = (own_back * inv[mine, :]).astype(BF16)
     if reduce_here:
         for copy in third:
             copy.wait_recv()
-        outs.append(pltpu.make_async_copy(gw_all, gw_hbm, out_sem.at[2]))
+        gw_out[...] = gw_all[...].astype(F32)
     else:
-        outs.append(pltpu.make_async_copy(gwf, gw_hbm, out_sem.at[2]))
-    outs[2].start()
+        gw_out[...] = gwf[...]
     sent = forward + early + exchange + backward
     if reduce_here:
         sent += first + second + third
     for copy in sent:
         copy.wait_send()
-    for copy in outs:
+
+
+def store_kernel(*refs):
+    sources, targets, sem = refs[:3], refs[3:6], refs[6]
+    copies = [pltpu.make_async_copy(sources[i], targets[i], sem.at[i]) for i in range(3)]
+    for copy in copies:
+        copy.start()
+    for copy in copies:
         copy.wait()
 
 
@@ -234,7 +237,7 @@
         pltpu.VMEM((own, width), BF16),
         pltpu.VMEM((n_rep, 1, own), jnp.int32),
         pltpu.VMEM(tile_values.shape, BF16),
-        pltpu.SMEM(tile_rows.shape, jnp.int32),
+        pltpu.SMEM((1, cap, span), jnp.int32),
         pltpu.SMEM(tile_counts.shape, jnp.int32),
         pltpu.VMEM((width, width), BF16),
         pltpu.VMEM((n_rep, own, width), BF16),
@@ -249,7 +252,6 @@
         pltpu.VMEM((slab, width), F32),
         pltpu.VMEM((span - 1, own, width), BF16),
         pltpu.VMEM((span - 1, own, width), BF16),
-        pltpu.VMEM((own, width), BF16),
         pltpu.VMEM((gw_rows, width), F32),
         pltpu.VMEM((gw_rows, width), BF16),
         pltpu.VMEM((GROUP - 1, max(piece, 16), width), BF16),
@@ -262,25 +264,37 @@
         dma((GROUP - 1,)), dma((GROUP - 1,)),
         dma((max(depth - 1, 1),)), dma((max(depth - 1, 1),)),
         dma((GROUP * n_rep - 1,)), dma((GROUP * n_rep - 1,)),
-        dma((3,)),
     ]
     anywhere = pl.BlockSpec(memory_space=pl.ANY)
+    in_vmem = pl.BlockSpec(memory_space=pltpu.VMEM)
+    in_hbm = pl.BlockSpec(memory_space=pltpu.HBM)
     activations, grad_weight, grad_features = pl.pallas_call(
         functools.partial(fused_kernel, dims),
         out_shape=(
             jax.ShapeDtypeStruct((own, width), BF16),
-            jax.ShapeDtypeStruct((width, width), BF16 if reduce_here else F32),
+            jax.ShapeDtypeStruct((width, width), F32),
             jax.ShapeDtypeStruct((own, width), BF16),
         ),
-        in_specs=[anywhere] * 7,
-        out_specs=(anywhere,) * 3,
+        in_specs=[in_hbm] * 7,
+        out_specs=(in_vmem,) * 3,
         scratch_shapes=scratch,
         compiler_params=pltpu.CompilerParams(
             collective_id=0, has_side_effects=True, vmem_limit_bytes=48 * 1024 * 1024),
-    )(features, degrees.reshape(1, own), tile_values, tile_rows, tile_counts, weight, cotangent)
-    if reduce_here:
-        grad_weight = grad_weight.astype(F32)
-    else:
+    )(*[pltpu.with_memory_space_constraint(x, pltpu.HBM) for x in (
+        features, degrees.reshape(1, own), tile_values, tile_rows.transpose(0, 2, 1),
+        tile_counts, weight, cotangent)])
+    activations, grad_weight, grad_features = pl.pallas_call(
+        store_kernel,
+        out_shape=(
+            jax.ShapeDtypeStruct((own, width), BF16),
+            jax.ShapeDtypeStruct((width, width), F32),
+            jax.ShapeDtypeStruct((own, width), BF16),
+        ),
+        in_specs=[anywhere] * 3,
+        out_specs=(in_hbm,) * 3,
+        scratch_shapes=[dma((3,))],
+    )(*[pltpu.with_memory_space_constraint(x, pltpu.VMEM) for x in (activations, grad_weight, grad_features)])
+    if not reduce_here:
         grad_weight = lax.psum(grad_weight, ("blk", "rep"))
     return (activations, grad_weight, grad_features)
 

time: 32.1 us -> 25.8 us (0.80)
  local copies, waits for them, and re-layouts: 6.13 us -> 0 us
  other arithmetic: 0.72 us -> 0 us
  Pallas kernels: 24.3 us -> 25 us
    unnamed x17 -> x0, local copies, waits for them, and re-layouts: 6.13 us -> none
    pallas_call x0 -> x1, Pallas kernels: none -> 0.77 us  [per_device(): pl.pallas_call(store_kernel, out_shape=(jax.ShapeDtypeStruct((own, width)...]
    convert_element_type x1 -> x0, other arithmetic: 0.72 us -> none  [per_device(): grad_weight = grad_weight.astype(F32)]
where the time goes in v2:
time: 25.8 us; the launch traced here: 25.6 us
  Pallas kernels  25 us (97%)
  between operations  0.64 us (2%)
    pallas_call x1, Pallas kernels, per_device(): pl.pallas_call(functools.partial(fused_kernel, dims), out_shape=(jax.Shap...  24.2 us
    pallas_call x1, Pallas kernels, per_device(): pl.pallas_call(store_kernel, out_shape=(jax.ShapeDtypeStruct((own, width)...  0.77 us

profile of v2, /device:TPU:0, one launch (start us, length us, event | category | flops | bytes accessed | tf_op | source)
XLA Modules:
  0.0 25.6 jit_solution(10778491231054310490)
XLA Ops:
  0.6 24.2 %shard_map.94 = (bf16[128,256]{1,0:T(8,128)(2,1)S(1)}, f32[256,256]{1,0:T(8,128)S(1)}, bf16[128,256]{1,0:T(8,128)(2,1)S(1)}) custom-call(bf16[128,256]{1,0:T(8,128)(2,1)} %refs_0_.1, s32[1,128]{1,0:T(1,128)} %bitcast.3, bf16[1,4,2,128,128]{4,3,2,1,0:T(8,128)(2,1)} %refs_2_.1, s32[1,2,4]{2,1,0:T(2,128)} %bitcast.2, s32[1,4]{1,0:T(1,128)} %refs_4_.1, ...), custom_call_target="tpu_custom_call" | custom-call | tf_op jit(solution)/shard_map/pallas_call | solution.py:271
  24.8 0.8 %shard_map.95 = (bf16[128,256]{1,0:T(8,128)(2,1)}, f32[256,256]{1,0:T(8,128)}, bf16[128,256]{1,0:T(8,128)(2,1)}) custom-call(bf16[128,256]{1,0:T(8,128)(2,1)S(1)} %get-tuple-element.6.refs_0_, f32[256,256]{1,0:T(8,128)S(1)} %get-tuple-element.7.refs_1_, bf16[128,256]{1,0:T(8,128)(2,1)S(1)} %get-tuple-element.8.refs_2_), custom_call_target="tpu_custom_call" | custom-call | tf_op jit(solution)/shard_map/pallas_call | solution.py:286
